TPU v7x, 32 devices: a whole 2x2x4 slice. The times are simulated.
32 devices in a mesh: dp: 16 (over z, x, core), tensor: 2 (over y).
Axes of the slice: x: 2, y: 2, z: 4, core: 2. Of those that a mesh axis runs over, the one named last changes fastest.
Arguments:
- block_input: bfloat16 [2, 16, 1024, 768], P(None, 'dp', 'tensor'), may hold values from -6 to 6
- cotangent: bfloat16 [2, 16, 1024, 768], P(None, 'dp', 'tensor'), may hold values from -6 to 6
- lengths: int32 [2, 16], P(None, 'dp'), may hold values from 128 to 1024, as said below
- ln1_gain: float32 [768], replicated, may hold values from 0.5 to 1.5
- ln1_bias: float32 [768], replicated, may hold values from -1.5 to 1.5
- ln2_gain: float32 [768], replicated, may hold values from 0.5 to 1.5
- ln2_bias: float32 [768], replicated, may hold values from -1.5 to 1.5
- w_query: bfloat16 [768, 768], P('dp', 'tensor'), may hold values from -0.21875 to 0.21875
- b_query: float32 [768], P('tensor'), may hold values from -3 to 3
- w_shared: bfloat16 [768, 128], P('dp'), may hold values from -0.21875 to 0.21875
- b_shared: float32 [128], replicated, may hold values from -3 to 3
- w_out: bfloat16 [768, 768], P('tensor', 'dp'), may hold values from -1.75 to 1.75
- b_out: float32 [768], replicated, may hold values from -3 to 3
- w_up: bfloat16 [768, 3072], P('dp', 'tensor'), may hold values from -0.21875 to 0.21875
- b_up: float32 [3072], P('tensor'), may hold values from -3 to 3
- w_down: bfloat16 [3072, 768], P('tensor', 'dp'), may hold values from -0.109375 to 0.109375
- b_down: float32 [768], replicated, may hold values from -3 to 3
Outputs:
- output: bfloat16 [2, 16, 1024, 768], P(None, 'dp', 'tensor')
- grad_input: bfloat16 [2, 16, 1024, 768], P(None, 'dp', 'tensor')
- grad_ln1_gain: float32 [768], replicated
- grad_ln1_bias: float32 [768], replicated
- grad_ln2_gain: float32 [768], replicated
- grad_ln2_bias: float32 [768], replicated
- grad_w_query: float32 [768, 768], P('dp', 'tensor')
- grad_b_query: float32 [768], P('tensor')
- grad_w_shared: float32 [768, 128], P('dp')
- grad_b_shared: float32 [128], replicated
- grad_w_out: float32 [768, 768], P('tensor', 'dp')
- grad_b_out: float32 [768], replicated
- grad_w_up: float32 [768, 3072], P('dp', 'tensor')
- grad_b_up: float32 [3072], P('tensor')
- grad_w_down: float32 [3072, 768], P('tensor', 'dp')
- grad_b_down: float32 [768], replicated
Inputs may be any that keep to these rules, and one draw needn't show every extreme that they name: `lengths`: each entry is the number of real tokens at the start of its padded sequence, the rest padding. For every sequence index s one of its 2 micro-batches has a length over 512, and one sequence of the whole batch has length exactly 1024.
All inputs are finite; a program needn't handle non-finite values.
Results may differ from a plain program's by a relative error of at most 0.011.
Values may be sent and summed in bfloat16 or wider, within the bound.
A program may use at most 192 MiB of HBM per device.

v0:
```python
from functools import partial

import jax
import jax.numpy as jnp
import numpy as np
from jax import lax
from jax.experimental import pallas as pl
from jax.experimental.pallas import tpu as pltpu
from jax.sharding import PartitionSpec as P

HEAD_DIM = 64
ROT = 16
MB = 2
QBLK = 512


EPS = 1e-05


def tables(count):
    places = jnp.arange(count).astype(jnp.float32)
    freqs = jnp.power(10000.0, -jnp.arange(ROT // 2).astype(jnp.float32) * 2.0 / ROT)
    angles = places[:, None] * freqs[None, :]
    return (jnp.cos(angles)[:, None, :], jnp.sin(angles)[:, None, :])


def rotate(vector, cosine, sine):
    first = vector[..., : ROT // 2]
    second = vector[..., ROT // 2 : ROT]
    return jnp.concatenate(
        [first * cosine - second * sine, second * cosine + first * sine, vector[..., ROT:]], axis=-1
    )


def unrotate(grad, cosine, sine):
    first = grad[..., : ROT // 2]
    second = grad[..., ROT // 2 : ROT]
    return jnp.concatenate(
        [first * cosine + second * sine, second * cosine - first * sine, grad[..., ROT:]], axis=-1
    )


def normalize(vector):
    centre = vector - jnp.mean(vector, axis=-1, keepdims=True)
    spread = jnp.mean(centre * centre, axis=-1, keepdims=True)
    scale = lax.rsqrt(spread + EPS)
    return (centre * scale, scale)


def norm_back(grad, normed, scale, gain):
    weighted = grad * gain
    return scale * (
        weighted
        - jnp.mean(weighted, axis=-1, keepdims=True)
        - normed * jnp.mean(weighted * normed, axis=-1, keepdims=True)
    )


def block_scores(rows, keys, start, limit, count):
    scores = jnp.einsum("qhd,kd->hqk", rows, keys, preferred_element_type=jnp.float32)
    row_pos = start + jnp.arange(QBLK)
    key_pos = jnp.arange(count)
    allowed = (key_pos[None, :] <= row_pos[:, None]) & (key_pos[None, :] < limit)
    return (scores, allowed[None])


def attend(queries, keys, values, limit):
    count = queries.shape[0]

    def block(start):
        rows = lax.dynamic_slice_in_dim(queries, start, QBLK, 0)
        scores, allowed = block_scores(rows, keys, start, limit, count)
        scores = jnp.where(allowed, scores, jnp.float32(-1e30))
        top = jnp.max(scores, axis=-1, keepdims=True)
        expo = jnp.exp(scores - top)
        total = jnp.sum(expo, axis=-1, keepdims=True)
        weights = (expo / total).astype(jnp.bfloat16)
        result = jnp.einsum("hqk,kd->qhd", weights, values, preferred_element_type=jnp.float32)
        return (result, (top + jnp.log(total))[..., 0])

    starts = jnp.arange(count // QBLK) * QBLK
    results, logsum = lax.map(block, starts)
    return (results.reshape(count, -1, HEAD_DIM), logsum)


def attend_back(queries, keys, values, limit, logsum, grad_out):
    count = queries.shape[0]

    def block(carry, item):
        start, block_logsum = item
        rows = lax.dynamic_slice_in_dim(queries, start, QBLK, 0)
        grads = lax.dynamic_slice_in_dim(grad_out, start, QBLK, 0)
        scores, allowed = block_scores(rows, keys, start, limit, count)
        probs = jnp.where(allowed, jnp.exp(scores - block_logsum[:, :, None]), 0.0)
        weights = probs.astype(jnp.bfloat16)
        dprobs = jnp.einsum("qhd,kd->hqk", grads, values, preferred_element_type=jnp.float32)
        delta = jnp.sum(probs * dprobs, axis=-1, keepdims=True)
        dscores = (probs * (dprobs - delta)).astype(jnp.bfloat16)
        drows = jnp.einsum("hqk,kd->qhd", dscores, keys, preferred_element_type=jnp.float32)
        dkeys = carry[0] + jnp.einsum(
            "hqk,qhd->kd", dscores, rows, preferred_element_type=jnp.float32
        )
        dvalues = carry[1] + jnp.einsum(
            "hqk,qhd->kd", weights, grads, preferred_element_type=jnp.float32
        )
        return ((dkeys, dvalues), drows)

    starts = jnp.arange(count // QBLK) * QBLK
    empty = jnp.zeros((count, HEAD_DIM), jnp.float32)
    (dkeys, dvalues), drows = lax.scan(block, (empty, empty), (starts, logsum))
    return (drows.reshape(count, -1, HEAD_DIM), dkeys, dvalues)


def fetch_each(w_query, w_shared, w_out, w_up, w_down):
    return (
        lax.all_gather(w_query, "dp", axis=0, tiled=True),
        lax.all_gather(w_shared, "dp", axis=0, tiled=True),
        lax.all_gather(w_out, "dp", axis=1, tiled=True),
        lax.all_gather(w_up, "dp", axis=0, tiled=True),
        lax.all_gather(w_down, "dp", axis=1, tiled=True),
    )


def reduce_each(step_grads):
    return (
        lax.psum_scatter(step_grads[0], "dp", scatter_dimension=0, tiled=True),
        lax.psum_scatter(step_grads[1], "dp", scatter_dimension=0, tiled=True),
        lax.psum_scatter(step_grads[2], "dp", scatter_dimension=1, tiled=True),
        lax.psum_scatter(step_grads[3], "dp", scatter_dimension=0, tiled=True),
        lax.psum_scatter(step_grads[4], "dp", scatter_dimension=1, tiled=True),
    )


def per_device(
    block_input,
    cotangent,
    lengths,
    ln1_gain,
    ln1_bias,
    ln2_gain,
    ln2_bias,
    w_query,
    b_query,
    w_shared,
    b_shared,
    w_out,
    b_out,
    w_up,
    b_up,
    w_down,
    b_down,
):
    shard_rows = block_input.shape[2]
    groups = lax.axis_size("tensor")
    rank = lax.axis_index("tensor")
    seq_len = shard_rows * groups
    tail_bias = b_out + b_down
    weight_sums = None
    cos_all, sin_all = tables(seq_len)
    own_pos = rank * shard_rows + jnp.arange(shard_rows)
    outputs = []
    input_grads = []
    sum_bq = jnp.zeros(b_query.shape, jnp.float32)
    sum_bkv = jnp.zeros(b_shared.shape, jnp.float32)
    sum_bup = jnp.zeros(b_up.shape, jnp.float32)
    sum_gain1 = jnp.zeros(ln1_gain.shape, jnp.float32)
    sum_shift1 = jnp.zeros(ln1_gain.shape, jnp.float32)
    sum_gain2 = jnp.zeros(ln1_gain.shape, jnp.float32)
    sum_shift2 = jnp.zeros(ln1_gain.shape, jnp.float32)
    sum_out = jnp.zeros(ln1_gain.shape, jnp.float32)
    for micro in range(MB):
        fetched = fetch_each(w_query, w_shared, w_out, w_up, w_down)
        wq_all, wkv_all, wo_all, wup_all, wdown_all = fetched
        limit = lengths[micro, 0]
        inputs = block_input[micro, 0].astype(jnp.float32)
        normed_one, scale_one = normalize(inputs)
        normed_two, scale_two = normalize(inputs)
        low_one = (normed_one * ln1_gain + ln1_bias).astype(jnp.bfloat16)
        low_two = (normed_two * ln2_gain + ln2_bias).astype(jnp.bfloat16)
        whole_one, whole_two = (
            lax.all_gather(low_one, "tensor", axis=0, tiled=True),
            lax.all_gather(low_two, "tensor", axis=0, tiled=True),
        )
        query_lin = jnp.dot(whole_one, wq_all, preferred_element_type=jnp.float32) + b_query
        query_lin = query_lin.reshape(seq_len, -1, HEAD_DIM)
        queries = (rotate(query_lin, cos_all, sin_all) * 0.125).astype(jnp.bfloat16)
        shared = jnp.dot(whole_one, wkv_all, preferred_element_type=jnp.float32) + b_shared
        keys = rotate(shared[:, None, :HEAD_DIM], cos_all, sin_all)[:, 0].astype(jnp.bfloat16)
        values = shared[:, HEAD_DIM:].astype(jnp.bfloat16)
        attended, logsum = attend(queries, keys, values, limit)
        attended_low = attended.reshape(seq_len, -1).astype(jnp.bfloat16)
        hidden = jnp.dot(whole_two, wup_all, preferred_element_type=jnp.float32) + b_up
        active = jax.nn.gelu(hidden, approximate=False).astype(jnp.bfloat16)
        partial_out = jnp.dot(attended_low, wo_all, preferred_element_type=jnp.float32) + jnp.dot(
            active, wdown_all, preferred_element_type=jnp.float32
        )
        branch = lax.psum_scatter(partial_out, "tensor", scatter_dimension=0, tiled=True)
        outputs.append((inputs + branch + tail_bias).astype(jnp.bfloat16))
        valid = (own_pos < limit).astype(jnp.float32)[:, None]
        upstream = cotangent[micro, 0].astype(jnp.float32) * valid
        whole_up = lax.all_gather(upstream.astype(jnp.bfloat16), "tensor", axis=0, tiled=True)
        sum_out = sum_out + jnp.sum(upstream, axis=0)
        grad_down = jnp.einsum("lf,ld->fd", active, whole_up, preferred_element_type=jnp.float32)
        dactive = jnp.einsum("ld,fd->lf", whole_up, wdown_all, preferred_element_type=jnp.float32)
        gelu_pull = jax.vjp(partial(jax.nn.gelu, approximate=False), hidden)[1]
        dhidden = gelu_pull(dactive)[0].astype(jnp.bfloat16)
        sum_bup = sum_bup + jnp.sum(dhidden.astype(jnp.float32), axis=0)
        grad_up = jnp.einsum("ld,lf->df", whole_two, dhidden, preferred_element_type=jnp.float32)
        dnormed_two = jnp.einsum("lf,df->ld", dhidden, wup_all, preferred_element_type=jnp.float32)
        dattended = jnp.einsum("ld,ed->le", whole_up, wo_all, preferred_element_type=jnp.float32)
        dattended = dattended.astype(jnp.bfloat16).reshape(seq_len, -1, HEAD_DIM)
        grad_out = jnp.einsum(
            "le,ld->ed", attended_low, whole_up, preferred_element_type=jnp.float32
        )
        dqueries, dkeys, dvalues = attend_back(queries, keys, values, limit, logsum, dattended)
        dquery_lin = (
            unrotate(dqueries * 0.125, cos_all, sin_all).reshape(seq_len, -1).astype(jnp.bfloat16)
        )
        dkey_lin = unrotate(dkeys[:, None, :], cos_all, sin_all)[:, 0]
        dshared = lax.psum(jnp.concatenate([dkey_lin, dvalues], axis=1), "tensor")
        dshared = dshared.astype(jnp.bfloat16)
        sum_bq = sum_bq + jnp.sum(dquery_lin.astype(jnp.float32), axis=0)
        sum_bkv = sum_bkv + jnp.sum(dshared.astype(jnp.float32), axis=0)
        grad_q = jnp.einsum("ld,le->de", whole_one, dquery_lin, preferred_element_type=jnp.float32)
        grad_kv = jnp.einsum("ld,lc->dc", whole_one, dshared, preferred_element_type=jnp.float32)
        dnormed_one = jnp.einsum(
            "le,de->ld", dquery_lin, wq_all, preferred_element_type=jnp.float32
        )
        dnormed_one, dnormed_two = (
            lax.psum_scatter(dnormed_one, "tensor", scatter_dimension=0, tiled=True),
            lax.psum_scatter(dnormed_two, "tensor", scatter_dimension=0, tiled=True),
        )
        own_shared = lax.dynamic_slice_in_dim(dshared, rank * shard_rows, shard_rows, 0)
        dnormed_one = dnormed_one + jnp.einsum(
            "lc,dc->ld", own_shared, wkv_all, preferred_element_type=jnp.float32
        )
        sum_gain1 = sum_gain1 + jnp.sum(dnormed_one * normed_one, axis=0)
        sum_shift1 = sum_shift1 + jnp.sum(dnormed_one, axis=0)
        sum_gain2 = sum_gain2 + jnp.sum(dnormed_two * normed_two, axis=0)
        sum_shift2 = sum_shift2 + jnp.sum(dnormed_two, axis=0)
        dinputs = (
            upstream
            + norm_back(dnormed_one, normed_one, scale_one, ln1_gain)
            + norm_back(dnormed_two, normed_two, scale_two, ln2_gain)
        )
        input_grads.append(dinputs.astype(jnp.bfloat16))
        step_grads = (grad_q, grad_kv, grad_out, grad_up, grad_down)
        step_grads = reduce_each(step_grads)
        if weight_sums is None:
            weight_sums = step_grads
        else:
            weight_sums = jax.tree.map(jnp.add, weight_sums, step_grads)
    output = jnp.stack(outputs, axis=0)[:, None]
    grad_input = jnp.stack(input_grads, axis=0)[:, None]
    sum_bq, sum_bkv, sum_bup = lax.psum((sum_bq, sum_bkv, sum_bup), "dp")
    sum_gain1, sum_shift1, sum_gain2, sum_shift2, sum_out = lax.psum(
        (sum_gain1, sum_shift1, sum_gain2, sum_shift2, sum_out), ("dp", "tensor")
    )
    grad_q, grad_kv, grad_o, grad_up, grad_down = weight_sums
    return (
        output,
        grad_input,
        sum_gain1,
        sum_shift1,
        sum_gain2,
        sum_shift2,
        grad_q,
        sum_bq,
        grad_kv,
        sum_bkv,
        grad_o,
        sum_out,
        grad_up,
        sum_bup,
        grad_down,
        sum_out,
    )


MESH = pl.DeviceIdType.MESH
BF = jnp.bfloat16
F32 = jnp.float32
LOG2E = 1.4426950408889634
LN2 = 0.6931471805599453
NEG = -1e30
ZC, XC, CC = 4, 2, 2
DMA = pltpu.SemaphoreType.DMA
VMEM = pltpu.VMEM
VMEM_LIMIT = (64 << 20) - 65536


def nn(a, b):
    return lax.dot_general(a, b, (((1,), (0,)), ((), ())), preferred_element_type=F32)


def nt(a, b):
    return lax.dot_general(a, b, (((1,), (1,)), ((), ())), preferred_element_type=F32)


def tn(a, b):
    return lax.dot_general(a, b, (((0,), (0,)), ((), ())), preferred_element_type=F32)


def eye(n):
    return (
        lax.broadcasted_iota(jnp.int32, (n, n), 0) == lax.broadcasted_iota(jnp.int32, (n, n), 1)
    ).astype(BF)


def flat(block):
    return block.reshape(-1, block.shape[-1])


class Place:
    def __init__(self):
        self.dp = lax.axis_index("dp")
        self.t = lax.axis_index("tensor")
        self.core = lax.rem(self.dp, CC)
        self.x = lax.rem(lax.div(self.dp, CC), XC)
        self.z = lax.div(self.dp, CC * XC)

    def at(self, z, x, core):
        return (z * XC + x) * CC + core

    def z_peer(self, d):
        return {"dp": self.at(lax.rem(self.z + d, ZC), self.x, self.core)}

    def x_peer(self):
        return {"dp": self.at(self.z, 1 - self.x, self.core)}

    def core_peer(self):
        return {"dp": self.at(self.z, self.x, 1 - self.core)}

    def y_peer(self):
        return {"tensor": 1 - self.t}

    def layer_peers(self):
        res = []
        for k in range(1, 8):
            x = 1 - self.x if k & 1 else self.x
            t = 1 - self.t if k & 2 else self.t
            core = 1 - self.core if k & 4 else self.core
            res.append({"dp": self.at(self.z, x, core), "tensor": t})
        return res

    def greet(self):
        bar = pltpu.get_barrier_semaphore()
        peers = [self.z_peer(d) for d in (1, 2, 3)] + self.layer_peers()
        for p in peers:
            pl.semaphore_signal(bar, inc=1, device_id=p, device_id_type=MESH)
        return bar, len(peers)


def remote(src, dst, ss, rs, peer):
    return pltpu.make_async_remote_copy(
        src_ref=src, dst_ref=dst, send_sem=ss, recv_sem=rs, device_id=peer, device_id_type=MESH
    )


def split_cols(width):
    a = (width // 128 + 1) // 2 * 128
    return ((0, a), (a, width - a))


class Gather:
    SLOTS = 3

    def __init__(self, place, pieces, sends, gots):
        self.p = place
        self.pieces = pieces
        self.sends, self.gots = sends, gots

    def own(self, c, h):
        p = self.p
        _, o, w, order = self.pieces[c][0][h]
        index = (p.z, p.x, p.core, slice(None), pl.ds(o, w))
        return self.pieces[c][1].at[(p.t,) + index if "y" in order else index]

    def copies(self, c, k):
        p = self.p
        every = slice(None)
        res = []
        for h, (src, o, w, order) in enumerate(self.pieces[c][0]):
            if k == 0:
                pairs = [(src, self.own(c, h), p.z_peer(d)) for d in (1, 2, 3)]
            elif k <= len(order):
                done = order[:k]
                index = (every, every if "x" in done else p.x, p.core, every, pl.ds(o, w))
                if "y" in order:
                    index = (every if "y" in done else p.t,) + index
                view = self.pieces[c][1].at[index]
                axis = order[k] if k < len(order) else "core"
                peers = {"x": p.x_peer(), "y": p.y_peer(), "core": p.core_peer()}
                pairs = [(view, view, peers[axis])]
            else:
                pairs = []
            for a, b, peer in pairs:
                res.append(remote(a, b, self.sends.at[c % self.SLOTS, k], self.gots.at[c, k], peer))
        return res

    def total(self, c, k):
        parts, out = self.pieces[c]
        z = pl.ds(0, 3) if k == 0 else slice(None)
        x = slice(None) if k > 1 else 0
        index = (z, x, 0)
        if "y" in parts[0][3]:
            index = (slice(None) if k > 2 else 0,) + index
        view = out.at[index]
        return remote(
            view, view, self.sends.at[c % self.SLOTS, k], self.gots.at[c, k], self.p.core_peer()
        )

    def run(self, ops):
        for op in ops:
            c, k = (op, -1) if isinstance(op, int) else op
            if k >= 0:
                self.total(c, k).wait()
            for cp in self.copies(c, k + 1):
                cp.start()


class AllSum:
    def __init__(self, place, buf, got, sems):
        self.p = place
        self.buf, self.got, self.sems = buf, got, sems

    def part(self, k):
        return (7, 3) if k else (0, 7)

    def start(self, k):
        peers = [self.p.z_peer(d) for d in (1, 2, 3)] if k else self.p.layer_peers()
        at, _ = self.part(k)
        for i, peer in enumerate(peers):
            got = self.got.at[at + i]
            remote(self.buf, got, self.sems.at[2 * k], self.sems.at[2 * k + 1], peer).start()

    def end(self, k):
        at, n = self.part(k)
        view = self.got.at[pl.ds(at, n)]
        whole = remote(
            view, view, self.sems.at[2 * k], self.sems.at[2 * k + 1], self.p.core_peer()
        )
        whole.wait()
        total = self.buf[...]
        for i in range(at, at + n):
            total = total + self.got[i]
        self.buf[...] = total


def normal_rows(rows):
    mean = jnp.mean(rows, axis=-1, keepdims=True)
    centre = rows - mean
    var = jnp.mean(centre * centre, axis=-1, keepdims=True)
    scale = lax.rsqrt(var + EPS)
    return centre * scale, scale


def rotate_t(v, cosine, sine):
    a, b = v[0:8], v[8:16]
    return jnp.concatenate([a * cosine - b * sine, b * cosine + a * sine, v[16:]], axis=0)


def unrotate_t(v, cosine, sine):
    a, b = v[0:8], v[8:16]
    return jnp.concatenate([a * cosine + b * sine, b * cosine - a * sine, v[16:]], axis=0)


def fill_bias(place, lens_ref, other_ref, own_ref, S):
    t = place.t
    for m in range(MB):
        limit = lens_ref[m]
        key = lax.broadcasted_iota(jnp.int32, (S, 128), 0)
        limit_other = jnp.where(t == 1, limit, 0)
        other_ref[m] = jnp.where(key < limit_other, 0.0, NEG).astype(F32)
        key = lax.broadcasted_iota(jnp.int32, (S, S), 0)
        row = lax.broadcasted_iota(jnp.int32, (S, S), 1)
        own = (key <= row) & (key + t * S < limit)
        own_ref[m] = jnp.where(own, 0.0, NEG).astype(F32)


def masked_rows(place_t, lens_ref, dy, start, S):
    m, off = divmod(start, S)
    pos = place_t * S + off + lax.broadcasted_iota(jnp.int32, (dy.shape[0], 1), 0)
    return jnp.where(pos < lens_ref[m], dy.astype(F32), 0.0)


class Reduce:
    SLOTS = 3

    def __init__(self, place, pieces, rc, r2a, r2b, r3, r4, sends, gots):
        self.p = place
        self.pieces = pieces
        self.rc, self.r2a, self.r2b, self.r3, self.r4 = rc, r2a, r2b, r3, r4
        self.sends, self.gots = sends, gots

    def part(self, c, h):
        r, n, o, w = self.pieces[c][1][h]
        _, first, _, second = self.pieces[c][3]
        o += first
        return (slice(r, r + n), slice(o, o + w)), (slice(0, n), slice(second, second + w))

    def wide(self, c):
        first = self.pieces[c][3][1]
        return slice(first, first + self.pieces[c][0].shape[-1])

    def sems(self, c, k):
        return self.sends.at[c % self.SLOTS, k], self.gots.at[c, k]

    def copies(self, c, k):
        p = self.p
        if k == 0:
            src = self.pieces[c][0].at[:, :, :, 1 - p.core]
            dst = self.rc.at[self.pieces[c][3][0], :, :, :, :, self.wide(c)]
            return [remote(src, dst, *self.sems(c, k), p.core_peer())]
        res = []
        a, _, b, _ = self.pieces[c][3]
        for h in (0, 1):
            here, there = self.part(c, h)
            if k == 1 and h == 0:
                src, dst = self.rc.at[(a, 1 - p.t, slice(None), slice(None)) + here], self.r2a
                todo = [(src, dst.at[(b, slice(None), slice(None)) + there], p.y_peer())]
            elif k == 1:
                src, dst = self.rc.at[(a, slice(None), slice(None), 1 - p.x) + here], self.r2b
                todo = [(src, dst.at[(b, slice(None), slice(None)) + there], p.x_peer())]
            elif k == 2:
                if h == 0:
                    src, peer = self.r2a.at[(b, slice(None), 1 - p.x) + there], p.x_peer()
                else:
                    src, peer = self.r2b.at[(b, 1 - p.t, slice(None)) + there], p.y_peer()
                todo = [(src, self.r3.at[(b, h, slice(None)) + there], peer)]
            else:
                todo = [
                    (
                        self.r3.at[(b, h, lax.rem(p.z + d, ZC)) + there],
                        self.r4.at[(b, h, d - 1) + there],
                        p.z_peer(d),
                    )
                    for d in (1, 2, 3)
                ]
            res += [remote(src, dst, *self.sems(c, k), peer) for src, dst, peer in todo]
        return res

    def total(self, c, k):
        cols = self.wide(c)
        every = slice(None)
        index = {
            0: (every, every, every, every, cols),
            1: (0, every, every, every, cols),
            2: (0, every, 0, every, cols),
            3: (0, pl.ds(0, 3), 0, every, cols),
        }[k]
        view = self.rc.at[(self.pieces[c][3][0],) + index]
        return remote(view, view, *self.sems(c, k), self.p.core_peer())

    def start(self, c, k):
        for cp in self.copies(c, k):
            cp.start()

    def add(self, c, k):
        p = self.p
        a, _, b, _ = self.pieces[c][3]
        if k == 1:
            cols = self.wide(c)
            mine = self.pieces[c][0][:, :, :, p.core].astype(F32)
            mine = mine + self.rc[a, :, :, :, :, cols].astype(F32)
            self.rc[a, :, :, :, :, cols] = mine.astype(BF)
            return
        sums = []
        for h in (0, 1):
            here, there = self.part(c, h)
            every = slice(None)
            if k == 2:
                if h == 0:
                    ref, mine = self.r2a, self.rc[(a, p.t, every, every) + here]
                else:
                    ref, mine = self.r2b, self.rc[(a, every, every, p.x) + here]
                at = (b, every, every) + there
                ref[at] = (mine.astype(F32) + ref[at].astype(F32)).astype(BF)
            elif k == 3:
                if h == 0:
                    mine = self.r2a[(b, every, p.x) + there]
                else:
                    mine = self.r2b[(b, p.t, every) + there]
                at = (b, h, every) + there
                self.r3[at] = (mine.astype(F32) + self.r3[at].astype(F32)).astype(BF)
            else:
                total = self.r3[(b, h, p.z) + there].astype(F32)
                for d in range(3):
                    total = total + self.r4[(b, h, d) + there].astype(F32)
                sums.append(total)
        if k == 4:
            self.pieces[c][2](sums)

    def run(self, ops):
        for c, k in ops:
            if k:
                self.total(c, k - 1).wait()
                self.add(c, k)
            if k < 4:
                self.start(c, k)


HEAD_OPS = (
    (0, 1),
    ((0, 0), (1, 0), 2),
    ((0, 1), (1, 1), 3),
    ((0, 2),),
    ((1, 2), 4),
    ((1, 3), (2, 0), (3, 0), 5),
)
ATTENTION_OPS = {
    0: ((2, 1), 6),
    2: ((4, 0),),
    4: ((3, 1), (5, 0), 7),
    5: ((2, 2),),
    7: ((3, 2), (2, 3), (4, 1), (6, 0), 8),
}
BACK_OPS = {
    0: ((3, 3), (4, 2), (5, 1), (7, 0)),
    3: ((4, 3), (5, 2), (6, 1), (8, 0)),
    5: ((5, 3), (6, 2), (7, 1)),
}
FFN_OPS = {
    0: (),
    1: ((6, 3), (7, 2), (8, 1)),
    2: ((7, 3), (8, 2)),
    3: ((8, 3),),
}


FFN_SUMS = {
    0: ((0, 1),),
    2: ((0, 2), (1, 1)),
    3: ((0, 3), (2, 1)),
    4: ((0, 4), (1, 2), (3, 1)),
    5: ((1, 3), (2, 2), (4, 1)),
}
BACK_SUMS = {
    6: ((1, 4), (2, 3), (3, 2), (5, 1)),
    8: ((2, 4), (3, 3), (4, 2), (6, 1)),
    9: ((7, 1),),
    10: ((3, 4), (4, 3), (5, 2)),
    11: ((7, 2), (8, 1), (6, 2)),
}
LAST_SUMS = (
    ((4, 4), (5, 3), (7, 3), (8, 2)),
    ((9, 1), (6, 3)),
    ((10, 1), (9, 2), (5, 4), (8, 3)),
    ((10, 2), (6, 4), (9, 3), (7, 4)),
    ((10, 3), (8, 4)),
    ((9, 4), (10, 4)),
)


def block_kernel(
    dims,
    x_hbm,
    dy_hbm,
    lens_ref,
    tab_ref,
    g1_ref,
    b1_ref,
    g2_ref,
    b2_ref,
    wq_in,
    bq_ref,
    wsh_in,
    bsh_ref,
    wout_in,
    bout_ref,
    wup_in,
    bup_ref,
    wdown_in,
    bdown_ref,
    out_hbm,
    gx_hbm,
    wf,
    grads,
    early,
    late,
    wsh,
    wq,
    wb,
    won,
    wv,
    ball,
    bcol,
    x_ref,
    dym,
    h1,
    h2,
    qt,
    att,
    da,
    tmp,
    acc,
    dh2,
    lse_ref,
    kvt,
    kvo,
    kc,
    vc,
    kt,
    vte,
    bias_o,
    bias_s,
    dkv,
    dkvs,
    dkvr,
    dkvn,
    gring,
    gb,
    gq,
    gkv,
    sums,
    early_in,
    late_in,
    rc,
    r2a,
    r2b,
    r3,
    r4,
    gsend,
    gsem,
    rsend,
    rsem,
    lsem,
    wsem,
    ysem,
    esem,
    asem,
):
    S, HT, NH, NF, T = dims["S"], dims["HT"], dims["NH"], dims["NF"], dims["T"]
    D = x_ref.shape[1]
    R = wq_in.shape[0]
    NB = S // 256
    p = Place()
    bar, npeers = p.greet()
    x_copy = pltpu.make_async_copy(x_hbm, x_ref, lsem.at[1])
    x_copy.start()
    dy_copy = pltpu.make_async_copy(dy_hbm, dym, lsem.at[0])
    dy_copy.start()

    def parts_of(ref, widths, orders):
        at = [sum(widths[:i]) for i in range(len(widths))]
        return [(ref.at[:, pl.ds(o, w)], o, w, order) for o, w, order in zip(at, widths, orders)]

    wide = [w for _, w in split_cols(HT)]
    pieces = [
        ([(wsh_in, 0, 128, "zx")], wsh),
        (parts_of(wq_in, wide, ("zxy", "zyx")), wq),
        (parts_of(wout_in, wide, ("zxy", "zyx")), wb),
    ]
    for f in range(NF):
        cols = pl.ds(256 * f, 256)
        parts = [(wup_in.at[:, cols], 0, 256, "zxy"), (wdown_in.at[:, cols], 256, 256, "zyx")]
        pieces.append((parts, wf.at[f]))
    g = Gather(p, pieces, gsend, gsem)
    pl.semaphore_wait(bar, npeers)
    g.run(HEAD_OPS[0])
    locals_ = [
        pltpu.make_async_copy(wsh_in, wsh.at[p.z, p.x, p.core], lsem.at[2]),
        pltpu.make_async_copy(wq_in, wq.at[p.t, p.z, p.x, p.core], lsem.at[3]),
        pltpu.make_async_copy(wout_in, wb.at[p.t, p.z, p.x, p.core], lsem.at[4]),
    ]
    for cp in locals_:
        cp.start()
    for c in range(3, len(pieces)):
        for h in (0, 1):
            pltpu.make_async_copy(pieces[c][0][h][0], g.own(c, h), lsem.at[5]).start()
    held = wf.at[:, 0, 0, 0, 0]
    locals_.append(pltpu.make_async_copy(held, held, lsem.at[5]))
    first = HT // 128
    rows_b = ball.shape[1]
    ball[p.t, 0:first, :] = bq_ref[...].reshape(first, 128)
    ball[p.t, first : first + 2 * NF, :] = bup_ref[...].reshape(2 * NF, 128)
    ball[p.t, first + 2 * NF :, :] = jnp.zeros((rows_b - first - 2 * NF, 128), F32)
    bias_copy = remote(ball.at[p.t], ball.at[p.t], ysem.at[0], ysem.at[1], p.y_peer())
    bias_copy.start()

    gain1, shift1, gain2, shift2 = (
        ref[...].reshape(1, D) for ref in (g1_ref, b1_ref, g2_ref, b2_ref)
    )

    def norm_block(i):
        rows = pl.ds(pl.multiple_of(i * 128, 128), 128)
        z, _ = normal_rows(x_ref[rows, :].astype(F32))
        h1[rows, :] = (z * gain1 + shift1).astype(BF)
        h2[rows, :] = (z * gain2 + shift2).astype(BF)

    half = T // 256
    x_copy.wait()
    pl.loop(0, half)(norm_block)
    for cp in locals_:
        cp.wait()
    g.run(HEAD_OPS[1])
    pl.loop(half, 2 * half)(norm_block)
    g.run(HEAD_OPS[2])
    fill_bias(p, lens_ref, bias_o, bias_s, S)
    for ref in (dkv, dh2, sums):
        ref[...] = jnp.zeros_like(ref)
    bias_copy.wait()
    nq = HT // 128
    for t in range(2):
        for j in range(nq):
            row = jnp.broadcast_to(ball[t, j : j + 1, :], (128, 128))
            bcol[(t * nq + j) * 128 : (t * nq + j + 1) * 128, :] = row.T
    bcol[2 * HT : 2 * HT + 128, :] = jnp.broadcast_to(bsh_ref[...].reshape(1, 128), (128, 128)).T
    g.run(HEAD_OPS[3])

    id256 = eye(256)
    cosine, sine = tab_ref[p.t, 0:8, :], tab_ref[p.t, 8:16, :]
    wsh_t = nt(eye(128), flat(wsh[...])).astype(BF)
    kv_copies = [
        remote(kvt.at[m], kvo.at[m], ysem.at[2 + 2 * m], ysem.at[3 + 2 * m], p.y_peer())
        for m in range(MB)
    ]
    for m in range(MB):
        kv = nt(wsh_t, h1[m * S : m * S + S, :]) + bcol[2 * HT : 2 * HT + 128, 0:1]
        kvt[m, 0:HEAD_DIM, :] = rotate_t(kv[0:HEAD_DIM], cosine, sine).astype(BF)
        kvt[m, HEAD_DIM:, :] = kv[HEAD_DIM:].astype(BF)
    g.run(HEAD_OPS[4])
    kv_copies[0].start()
    dy_copy.wait()
    for b in range(T // 256):
        rows = slice(b * 256, b * 256 + 256)
        dy = masked_rows(p.t, lens_ref, dym[rows, :], b * 256, S)
        dym[rows, :] = dy.astype(BF)
        sums[6:7, :] += jnp.sum(dy, axis=0, keepdims=True)
    g.run(HEAD_OPS[5])

    for t in range(2):
        wq_t = nt(eye(HT), flat(wq[t])).astype(BF)
        for m in range(MB):
            cols = slice(m * S, m * S + S)
            q = nt(wq_t, h1[cols, :])
            for h in range(HT // HEAD_DIM):
                base = t * HT + h * HEAD_DIM
                qh = q[h * HEAD_DIM : (h + 1) * HEAD_DIM] + bcol[base : base + HEAD_DIM, 0:1]
                qh = rotate_t(qh, cosine, sine) * (0.125 * LOG2E)
                qt[base : base + HEAD_DIM, cols] = qh.astype(BF)

    def both_halves(m):
        kv_copies[m].wait()
        for part, src in ((0, kvo), (1, kvt)):
            keys = slice(part * S, part * S + S)
            kt[m, :, keys] = src[m, 0:HEAD_DIM, :]
            vte[m, 0:HEAD_DIM, keys] = src[m, HEAD_DIM:, :]
        vte[m, HEAD_DIM:, :] = (
            lax.broadcasted_iota(jnp.int32, (16, 2 * S), 0) == 0
        ).astype(BF)
        for b in range(2 * NB):
            blk = slice(b * 256, b * 256 + 256)
            kc[m, blk, :] = nt(id256, kt[m, :, blk]).astype(BF)
            vc[m, blk, :] = nt(id256, vte[m, 0:HEAD_DIM, blk]).astype(BF)

    both_halves(0)

    def spots(i, group, by_thirds=False):
        res = []
        for u in range(group):
            j = i * group + u
            m, h = lax.div(j, NH), lax.rem(j, NH)
            if by_thirds:
                k = lax.div(h, 2)
                h = lax.rem(k, 2) * (NH // 2) + lax.div(k, 2) * 2 + u
                j = m * NH + h
            head = pl.ds(pl.multiple_of(h * HEAD_DIM, HEAD_DIM), HEAD_DIM)
            for r in range(NB):
                cols = pl.ds(pl.multiple_of(m * S + r * 256, 256), 256)
                res.append((j, m, head, cols, S + 256 * (r + 1), r))
        return res

    def scores(m, q, nk, r):
        s = nn(kc[m, 0:nk, :], q)
        wide = slice(r * 256, r * 256 + 256)
        other = bias_o[m]
        other = jnp.concatenate([other, other], axis=1)
        return jnp.concatenate([s[0:S] + other, s[S:nk] + bias_s[m, 0 : nk - S, wide]], axis=0)

    group = 3

    @pl.loop(0, MB * NH // group)
    def _(i):
        for m in range(1, MB):
            pl.when(i == (m - 1) * NH // group)(kv_copies[m].start)
            pl.when(i == m * NH // group)(partial(both_halves, m))
        for at, ops in ATTENTION_OPS.items():
            pl.when(i == at)(partial(g.run, ops))
        todo = spots(i, group)
        sc = [scores(m, qt[head, cols], nk, r) for _, m, head, cols, nk, r in todo]
        tops = [jnp.max(s, axis=0, keepdims=True) for s in sc]
        ex = [jnp.exp2(s - top).astype(BF) for s, top in zip(sc, tops)]
        for (j, m, head, cols, nk, r), e, top in zip(todo, ex, tops):
            o = nn(vte[m, :, 0:nk], e)
            total = o[HEAD_DIM : HEAD_DIM + 1]
            att[head, cols] = (o[0:HEAD_DIM] * (1.0 / total)).astype(BF)
            lse_ref[j, :, r * 256 : r * 256 + 256] = top + jnp.log2(total)

    for t in range(2):
        won[t * HT : (t + 1) * HT, :] = nt(eye(HT), flat(wb[t])).astype(BF)

    def load(f, slot):
        return pltpu.make_async_copy(wf.at[f], wv.at[slot], wsem.at[slot])

    for b in range(T // 256):
        rows = slice(b * 256, b * 256 + 256)
        tmp[rows, :] = nt(id256, att[:, rows]).astype(BF)
    tail_bias = (bout_ref[...] + bdown_ref[...]).reshape(1, D)
    acc[...] = x_ref[...].astype(F32) + tail_bias + nn(tmp[...], won[...])
    for t in range(2):
        cols = slice(t * HT, (t + 1) * HT)
        gb[t] = tn(dym[...], tmp[:, cols]).astype(BF).reshape(ZC, XC, CC, R, HT)

    def put(*firsts):
        def store(parts):
            for o, v in zip(firsts, parts):
                grads[:, o : o + v.shape[1]] = v

        return store

    at_out, at_up, at_down = HT + 128, 2 * HT + 128, 2 * HT + 128 + 256 * NF
    thirds = HT // 128

    def by_cols(*widths):
        at = [sum(widths[:i]) for i in range(len(widths))]
        return [(0, R, o, w) for o, w in zip(at, widths)]

    def put_rows(first):
        def store(parts):
            r = 0
            for v in parts:
                grads[r : r + v.shape[0], first : first + 128] = v
                r += v.shape[0]

        return store

    by_rows = [(0, 32, 0, 128), (32, R - 32, 0, 128)]
    sums_of = [(gb, by_cols(*wide), put(at_out, at_out + wide[0]), (0, 0, 0, 0))]
    for f in range(NF):
        store = put(at_up + 256 * f, at_down + 256 * f)
        sums_of.append((gring.at[f % 3], by_cols(256, 256), store, (1 + f, 0, 1 + f, 0)))
    for k in range(thirds + 1):
        store = put_rows(128 * k)
        slot = (NF + 1, 128 * k, NF + 1 + k // 2, 128 * (k % 2))
        sums_of.append((gq.at[k] if k < thirds else gkv, by_rows, store, slot))
    red = Reduce(p, sums_of, rc, r2a, r2b, r3, r4, rsend, rsem)
    last = NF + 1
    red.run([(0, 0)])

    n = D // 128
    early_sum = AllSum(p, early, early_in, esem)
    da[...] = nt(won[...], dym[...]).astype(BF)
    back = 2
    dkv_copies = [
        remote(dkvs.at[m], dkvr.at[m], ysem.at[6 + 2 * m], ysem.at[7 + 2 * m], p.y_peer())
        for m in range(MB)
    ]

    def send_dkv(m):
        dkvs[m] = dkv[m, 0:S, :].astype(BF)
        dkv_copies[m].start()

    def query_third(k):
        for t in range(2):
            at = t * HT + 128 * k
            for b in range(T // 256):
                rows = slice(b * 256, b * 256 + 256)
                tmp[rows, at : at + 128] = nt(id256, qt[at : at + 128, rows]).astype(BF)
            v = tn(h1[...], tmp[:, at : at + 128]).astype(BF)
            gq[k, t] = v.reshape(ZC, XC, CC, R, 128)
        red.run([(last + k, 0)])

    def own_dkv(m):
        dkv_copies[m].wait()
        both = (dkv[m, S : 2 * S, :] + dkvr[m].astype(F32)).T
        dk = unrotate_t(both[0:HEAD_DIM], cosine, sine) * LN2
        both = jnp.concatenate([dk, both[HEAD_DIM:]], axis=0).astype(BF)
        for b in range(NB):
            rows = slice(m * S + b * 256, m * S + b * 256 + 256)
            dkvn[rows, :] = nt(id256, both[:, b * 256 : b * 256 + 256]).astype(BF)

    def early_next():
        early_sum.end(0)
        early_sum.start(1)

    def back_step(i):
        for at, ops in BACK_OPS.items():
            pl.when(i == at)(partial(g.run, ops))
        pl.when(i == NH // back + 2)(early_next)
        pl.when(i == NH // back + 3)(partial(own_dkv, 0))
        for at, ops in BACK_SUMS.items():
            pl.when(i == at)(partial(red.run, ops))
        for k in range(thirds - 1):
            at = MB * NH // back - 2 * (thirds - 1 - k)
            pl.when(i == at)(partial(query_third, k))
        todo = spots(i, back, True)
        qs = [qt[head, cols] for _, m, head, cols, nk, r in todo]
        das = [da[head, cols] for _, m, head, cols, nk, r in todo]
        sc = [scores(m, q, nk, r) for (_, m, head, cols, nk, r), q in zip(todo, qs)]
        dp = [nn(vc[m, 0:nk, :], d) for (_, m, head, cols, nk, r), d in zip(todo, das)]
        pr, ds = [], []
        for (j, m, head, cols, nk, r), d, s, dpj in zip(todo, das, sc, dp):
            delta = jnp.sum(d.astype(F32) * att[head, cols].astype(F32), axis=0, keepdims=True)
            w = jnp.exp2(s - lse_ref[j, :, r * 256 : r * 256 + 256])
            pr.append(w.astype(BF))
            ds.append((w * (dpj - delta)).astype(BF))
        for (j, m, head, cols, nk, r), d in zip(todo, ds):
            wide = slice(r * 256, r * 256 + 256)
            dq = nn(kt[m, :, 0:nk], d)
            dq = unrotate_t(dq, tab_ref[p.t, 0:8, wide], tab_ref[p.t, 8:16, wide])
            qt[head, cols] = (dq * 0.125).astype(BF)
        m = todo[0][1]
        for blk in range(NB):
            lo = 0 if blk == 0 else S + 256 * blk
            hi = S + 256 * (blk + 1)
            left, right = [], []
            for u, (_, _, _, _, nk, r) in enumerate(todo):
                if nk >= hi:
                    zero = jnp.zeros_like(qs[u])
                    left += [ds[u][lo:hi], pr[u][lo:hi]]
                    right += [
                        jnp.concatenate([qs[u], zero], axis=0),
                        jnp.concatenate([zero, das[u]], axis=0),
                    ]
            dkv[m, lo:hi, :] += nt(
                jnp.concatenate(left, axis=1), jnp.concatenate(right, axis=1)
            )

    per = NH // back
    lead = per * (MB - 1)
    def ffn_step(f):
        slot = lax.rem(f, 2)
        load(f, slot).wait()
        for k in range(NF - 1):

            @pl.when(f == k)
            def _():
                g.run(FFN_OPS.get(k, ()))
                load(k + 1, (k + 1) % 2).start()

        for k, ops in FFN_SUMS.items():
            pl.when(f == k)(partial(red.run, ops))
        wu = [flat(wv[slot, t, :, :, :, :, 0:256]) for t in range(2)]
        wd = [flat(wv[slot, t, :, :, :, :, 256:512]) for t in range(2)]
        gslot = lax.rem(f, 3)
        hid = [nn(h2[...], wu[t]) for t in range(2)]
        dact = [nn(dym[...], wd[t]) for t in range(2)]
        act, dhid = [], []
        for t in range(2):
            row = jnp.concatenate(
                [ball[t, pl.ds(first + 2 * f, 1), :], ball[t, pl.ds(first + 2 * f + 1, 1), :]],
                axis=1,
            )
            u = hid[t] + row
            cdf = 0.5 + 0.5 * lax.erf(u * 0.7071067811865476)
            dens = jnp.exp(-0.5 * u * u) * 0.3989422804014327
            act.append((u * cdf).astype(BF))
            d = (dact[t] * (cdf + u * dens)).astype(BF)
            dhid.append(d)
            total = jnp.sum(d.astype(F32), axis=0, keepdims=True)
            for j in (0, 1):
                at = D // 128 + 4 * f + 2 * t + j
                early[pl.ds(at, 1), :] = total[:, 128 * j : 128 * j + 128]
        acc[...] += nt(act[0], wd[0]) + nt(act[1], wd[1])
        dh2[...] += nt(dhid[0], wu[0]) + nt(dhid[1], wu[1])
        for t in range(2):
            gd = tn(dym[...], act[t]).astype(BF)
            gring[gslot, t, :, :, :, :, 256:512] = gd.reshape(ZC, XC, CC, R, 256)
            gu = tn(h2[...], dhid[t]).astype(BF)
            gring[gslot, t, :, :, :, :, 0:256] = gu.reshape(ZC, XC, CC, R, 256)
        for k in range(NF):
            pl.when(f == k)(partial(red.run, [(1 + k, 0)]))

    out_copy = pltpu.make_async_copy(h2, out_hbm, lsem.at[6])

    def after_lead():
        for m in range(MB - 1):
            send_dkv(m)
        load(0, 0).start()

    def after_ffn():
        h2[...] = acc[...].astype(BF)
        out_copy.start()
        early[0:n, :] = sums[6:7, :].reshape(n, 128)
        early[n + 4 * NF :, :] = jnp.zeros((early.shape[0] - n - 4 * NF, 128), F32)
        early_sum.start(0)

    @pl.loop(0, per * MB + NF)
    def _(i):
        pl.when(i == lead)(after_lead)
        pl.when(i == lead + NF)(after_ffn)
        in_ffn = (i >= lead) & (i < lead + NF)
        pl.when(in_ffn)(lambda: ffn_step(i - lead))
        pl.when(jnp.logical_not(in_ffn))(lambda: back_step(jnp.where(i < lead, i, i - NF)))

    send_dkv(MB - 1)
    query_third(thirds - 1)
    red.run(LAST_SUMS[0])

    wqf = [flat(wq[t]) for t in range(2)]
    wshf = flat(wsh[...])

    def input_grad(b):
        rows = slice(b * 256, b * 256 + 256)
        dq, dkvb = tmp[rows, :], dkvn[rows, :]
        dh1 = nt(dq[:, 0:HT], wqf[0]) + nt(dq[:, HT:], wqf[1]) + nt(dkvb, wshf)
        dh2b = dh2[rows, :]
        z, scale = normal_rows(x_ref[rows, :].astype(F32))
        dy = dym[rows, :].astype(F32)
        e = dh1 * gain1 + dh2b * gain2
        back_in = scale * (
            e - jnp.mean(e, axis=-1, keepdims=True) - z * jnp.mean(e * z, axis=-1, keepdims=True)
        )
        tmp[rows, :] = (dy + back_in).astype(BF)
        for k, v in enumerate((dh1 * z, dh1, dh2b * z, dh2b, dq.astype(F32))):
            sums[k : k + 1, :] += jnp.sum(v, axis=0, keepdims=True)
        sums[5:6, 0:128] += jnp.sum(dkvb.astype(F32), axis=0, keepdims=True)

    input_grad(0)
    own_dkv(1)
    red.run(LAST_SUMS[1])
    gkvs = tn(h1[...], dkvn[...]).astype(BF).reshape(ZC, XC, CC, R, 128)
    for t in range(2):
        gkv[t] = gkvs
    red.run([(last + thirds, 0)])
    input_grad(1)
    input_grad(2)
    red.run(LAST_SUMS[2])
    input_grad(3)
    for k in range(5):
        late[k * n : k * n + n, :] = sums[k : k + 1, :].reshape(n, 128)
    late[5 * n : 5 * n + 1, :] = sums[5:6, 0:128]
    late[5 * n + 1 :, :] = jnp.zeros((late.shape[0] - 5 * n - 1, 128), F32)
    late_sum = AllSum(p, late, late_in, asem)
    late_sum.start(0)
    gx_copy = pltpu.make_async_copy(tmp, gx_hbm, lsem.at[7])
    gx_copy.start()
    red.run(LAST_SUMS[3])
    late_sum.end(0)
    late_sum.start(1)
    early_sum.end(1)
    red.run(LAST_SUMS[4])
    red.run(LAST_SUMS[5])
    late_sum.end(1)
    out_copy.wait()
    gx_copy.wait()


def finish_kernel(dims, out_in, gx_in, grads_in, early, late, *refs):
    (out, gx, g1, b1, g2, b2, gq, bq, gkv, bkv, go, bo, gup, bup, gdn, bd) = refs[:16]
    held, grads, sem = refs[16:]
    HT, NF = dims["HT"], dims["NF"]
    there = [
        pltpu.make_async_copy(grads_in, grads, sem.at[0]),
        pltpu.make_async_copy(out_in, held.at[0], sem.at[1]),
        pltpu.make_async_copy(gx_in, held.at[1], sem.at[2]),
    ]
    for cp in there:
        cp.start()
    parts, at = [], 0
    for k, ref in enumerate((gq, gkv, go, gup, gdn)):
        cols = pl.ds(at, ref.shape[1])
        parts.append(pltpu.make_async_copy(grads.at[:, cols], ref, sem.at[3 + k]))
        at += ref.shape[1]
    back = [
        parts,
        [pltpu.make_async_copy(held.at[0], out, sem.at[8])],
        [pltpu.make_async_copy(held.at[1], gx, sem.at[9])],
    ]
    t = lax.axis_index("tensor")
    n = g1.shape[0] // 128
    for k, ref in enumerate((g1, b1, g2, b2)):
        ref[...] = late[k * n : k * n + n, :].reshape(n * 128)
    half = HT // 128
    bq[...] = late[pl.ds(4 * n + half * t, half), :].reshape(HT)
    bkv[...] = late[5 * n : 5 * n + 1, :].reshape(128)
    total = early[0:n, :].reshape(n * 128)
    bo[...] = total
    bd[...] = total
    for cp, then in zip(there, back):
        cp.wait()
        for after in then:
            after.start()
    for f in range(NF):
        for j in (0, 1):
            at = 256 * f + 128 * j
            bup[at : at + 128] = early[pl.ds(n + 4 * f + 2 * t + j, 1), :].reshape(128)
    for then in back:
        for cp in then:
            cp.wait()


def angle_table(S):
    places = np.arange(2 * S, dtype=np.float64)
    freqs = 10000.0 ** (-np.arange(ROT // 2) * 2.0 / ROT)
    angles = (places[:, None] * freqs[None, :]).astype(np.float32).astype(np.float64)
    tab = np.concatenate([np.cos(angles).T, np.sin(angles).T], axis=0).astype(np.float32)
    return tab.reshape(ROT, 2, S).transpose(1, 0, 2)


def token_plan(
    block_input,
    cotangent,
    lengths,
    ln1_gain,
    ln1_bias,
    ln2_gain,
    ln2_bias,
    w_query,
    b_query,
    w_shared,
    b_shared,
    w_out,
    b_out,
    w_up,
    b_up,
    w_down,
    b_down,
):
    S, D = block_input.shape[2:]
    R, HT = w_query.shape
    FT = w_up.shape[1]
    NF, T, NH = FT // 256, MB * S, 2 * HT // HEAD_DIM
    dims = dict(S=S, HT=HT, NF=NF, T=T, NH=NH)
    plane = (ZC, XC, CC, R)
    full = (2,) + plane
    t = lax.axis_index("tensor")

    def s(shape, dtype):
        return jax.ShapeDtypeStruct(shape, dtype)

    vm = pl.BlockSpec(memory_space=VMEM)
    hbm = pl.BlockSpec(memory_space=pl.ANY)
    smem = pl.BlockSpec(memory_space=pltpu.SMEM)

    nb = HT // 128 + 2 * NF + 1
    n_gather, n_reduce = NF + 3, NF + 2 + HT // 128
    n_early, n_late = 8 * ((D // 128 + 4 * NF + 7) // 8), 8 * ((5 * (D // 128) + 8) // 8)
    n_grads = 2 * HT + 128 + 2 * FT

    outs = pl.pallas_call(
        partial(block_kernel, dims),
        out_shape=[
            s((T, D), BF),
            s((T, D), BF),
            s((NF,) + full + (512,), BF),
            s((R, n_grads), F32),
            s((n_early, 128), F32),
            s((n_late, 128), F32),
        ],
        in_specs=[hbm, hbm, smem] + [vm] * 15,
        out_specs=[hbm] * 3 + [vm] * 3,
        scratch_shapes=[
            VMEM(plane + (128,), BF),
            VMEM(full + (HT,), BF),
            VMEM(full + (HT,), BF),
            VMEM((2 * HT, D), BF),
            VMEM((2,) + full + (512,), BF),
            VMEM((2, nb, 128), F32),
            VMEM((2 * HT + 128, 128), F32),
            VMEM((T, D), BF),
            VMEM((T, D), BF),
            VMEM((T, D), BF),
            VMEM((T, D), BF),
            VMEM((D, T), BF),
            VMEM((D, T), BF),
            VMEM((D, T), BF),
            VMEM((T, D), BF),
            VMEM((T, D), F32),
            VMEM((T, D), F32),
            VMEM((MB * NH, 1, S), F32),
            VMEM((MB, 128, S), BF),
            VMEM((MB, 128, S), BF),
            VMEM((MB, 2 * S, HEAD_DIM), BF),
            VMEM((MB, 2 * S, HEAD_DIM), BF),
            VMEM((MB, HEAD_DIM, 2 * S), BF),
            VMEM((MB, HEAD_DIM + 16, 2 * S), BF),
            VMEM((MB, S, 128), F32),
            VMEM((MB, S, S), F32),
            VMEM((MB, 2 * S, 128), F32),
            VMEM((MB, S, 128), BF),
            VMEM((MB, S, 128), BF),
            VMEM((T, 128), BF),
            VMEM((3,) + full + (512,), BF),
            VMEM(full + (HT,), BF),
            VMEM((HT // 128,) + full + (128,), BF),
            VMEM(full + (128,), BF),
            VMEM((8, D), F32),
            VMEM((10, n_early, 128), F32),
            VMEM((10, n_late, 128), F32),
            VMEM((NF + 2, 2, ZC, XC, R, 512), BF),
            VMEM((NF + 3, ZC, XC, R, 256), BF),
            VMEM((NF + 3, 2, ZC, R, 256), BF),
            VMEM((NF + 3, 2, ZC, R, 256), BF),
            VMEM((NF + 3, 2, 3, R, 256), BF),
            DMA((Gather.SLOTS, 4)),
            DMA((n_gather, 4)),
            DMA((Reduce.SLOTS, 4)),
            DMA((n_reduce, 4)),
            DMA((8,)),
            DMA((2,)),
            DMA((6 + 2 * MB,)),
            DMA((4,)),
            DMA((4,)),
        ],
        compiler_params=pltpu.CompilerParams(
            vmem_limit_bytes=VMEM_LIMIT, collective_id=0, has_side_effects=True
        ),
        name="block",
    )(
        block_input.reshape(T, D),
        cotangent.reshape(T, D),
        lengths.reshape(MB),
        jnp.asarray(angle_table(S)),
        ln1_gain,
        ln1_bias,
        ln2_gain,
        ln2_bias,
        w_query,
        b_query,
        w_shared,
        b_shared,
        w_out.T,
        b_out,
        w_up,
        b_up,
        w_down.T,
        b_down,
    )
    out, gx, _, grads, early, late = outs
    vec = s((D,), F32)
    shapes = [s((T, D), BF), s((T, D), BF), vec, vec, vec, vec, s((R, HT), F32), s((HT,), F32)]
    shapes += [s((R, 128), F32), s((128,), F32), s((R, HT), F32), vec, s((R, FT), F32)]
    shapes += [s((FT,), F32), s((R, FT), F32), vec]
    outs = pl.pallas_call(
        partial(finish_kernel, dims),
        out_shape=shapes,
        in_specs=[hbm, hbm, hbm, vm, vm],
        out_specs=[hbm if len(shape.shape) > 1 else vm for shape in shapes],
        scratch_shapes=[VMEM((2, T, D), BF), VMEM((R, n_grads), F32), DMA((10,))],
        compiler_params=pltpu.CompilerParams(vmem_limit_bytes=VMEM_LIMIT),
        name="finish",
    )(out, gx, grads, early, late)
    res = list(outs)
    res[0] = res[0].reshape(block_input.shape)
    res[1] = res[1].reshape(block_input.shape)
    res[10] = res[10].T
    res[14] = res[14].T
    return tuple(res)


def fits_token_plan(mesh):
    return dict(mesh.shape) == {"dp": ZC * XC * CC, "tensor": 2}


def solution(mesh):
    in_specs = (
        P(None, "dp", "tensor", None),
        P(None, "dp", "tensor", None),
        P(None, "dp"),
        P(),
        P(),
        P(),
        P(),
        P("dp", "tensor"),
        P("tensor"),
        P("dp", None),
        P(),
        P("tensor", "dp"),
        P(),
        P("dp", "tensor"),
        P("tensor"),
        P("tensor", "dp"),
        P(),
    )
    out_specs = (
        P(None, "dp", "tensor", None),
        P(None, "dp", "tensor", None),
        P(),
        P(),
        P(),
        P(),
        P("dp", "tensor"),
        P("tensor"),
        P("dp", None),
        P(),
        P("tensor", "dp"),
        P(),
        P("dp", "tensor"),
        P("tensor"),
        P("tensor", "dp"),
        P(),
    )
    step = token_plan if fits_token_plan(mesh) else per_device
    return jax.shard_map(
        step, mesh=mesh, in_specs=in_specs, out_specs=out_specs, check_vma=False
    )
```

profile of v0, /device:TPU:0, one launch (start us, length us, event | category | flops | bytes accessed | tf_op | source)
XLA Modules:
  0.0 154.7 jit_solution(1316890088108300783)
XLA Ops:
  0.7 149.1 %block.1 = (bf16[1024,768]{1,0:T(8,128)(2,1)}, bf16[1024,768]{1,0:T(8,128)(2,1)}, bf16[6,2,4,2,2,48,512]{6,5,4,3,2,1,0:T(8,128)(2,1)}, f32[48,3968]{1,0:T(8,128)}, f32[32,128]{1,0:T(8,128)}, /*index=5*/f32[32,128]{1,0:T(8,128)}) custom-call(bf16[1024,768]{1,0:T(8,128)(2,1)} %bitcast.13, bf16[1024,768]{1,0:T(8,128)(2,1)} %bitcast.14, s32[2]{0:T(128)} %bitcast.17, ...), custom_call_target="tpu_custom_call" | custom-call | tf_op jit(solution)/shard_map/block/pallas_call | solution.py:1242
  149.7 4.8 %finish.1 = (bf16[1024,768]{1,0:T(8,128)(2,1)}, bf16[1024,768]{1,0:T(8,128)(2,1)}, f32[768]{0:T(1024)}, f32[768]{0:T(1024)}, f32[768]{0:T(1024)}, /*index=5*/f32...) custom-call(bf16[1024,768]{1,0:T(8,128)(2,1)} %get-tuple-element.37., ...), custom_call_target="tpu_custom_call" | custom-call | tf_op jit(solution)/shard_map/finish/pallas_call | solution.py:1336
where the time goes:
time: 155 us
  Pallas kernels  154 us (99%)
    pallas_call x1, Pallas kernels, token_plan(): pl.pallas_call(partial(block_kernel, dims), out_shape=[s((T, D), BF), s((...  149 us
    pallas_call x1, Pallas kernels, token_plan(): pl.pallas_call(partial(finish_kernel, dims), out_shape=shapes, in_specs=[...  4.81 us

commit v1 on v0

--- a/solution.py
+++ b/solution.py
@@ -609,22 +609,24 @@
     ((1, 3), (2, 0), (3, 0), 5),
 )
 ATTENTION_OPS = {
-    0: ((2, 1), 6),
+    0: (6,),
+    1: ((2, 1),),
     2: ((4, 0),),
     4: ((3, 1), (5, 0), 7),
     5: ((2, 2),),
-    7: ((3, 2), (2, 3), (4, 1), (6, 0), 8),
+    7: ((2, 3), (4, 1), (6, 0), 8),
 }
 BACK_OPS = {
-    0: ((3, 3), (4, 2), (5, 1), (7, 0)),
-    3: ((4, 3), (5, 2), (6, 1), (8, 0)),
-    5: ((5, 3), (6, 2), (7, 1)),
+    0: ((3, 2), (4, 2), (5, 1), (7, 0)),
+    3: ((3, 3), (4, 3), (5, 2), (6, 1), (8, 0)),
+    5: ((5, 3), (7, 1)),
 }
 FFN_OPS = {
-    0: (),
+    0: ((6, 2),),
     1: ((6, 3), (7, 2), (8, 1)),
-    2: ((7, 3), (8, 2)),
-    3: ((8, 3),),
+    2: ((7, 3),),
+    3: ((8, 2),),
+    4: ((8, 3),),
 }
 
 
@@ -1151,23 +1153,21 @@
     (out, gx, g1, b1, g2, b2, gq, bq, gkv, bkv, go, bo, gup, bup, gdn, bd) = refs[:16]
     held, grads, sem = refs[16:]
     HT, NF = dims["HT"], dims["NF"]
-    there = [
-        pltpu.make_async_copy(grads_in, grads, sem.at[0]),
-        pltpu.make_async_copy(out_in, held.at[0], sem.at[1]),
-        pltpu.make_async_copy(gx_in, held.at[1], sem.at[2]),
-    ]
-    for cp in there:
-        cp.start()
+    there = [pltpu.make_async_copy(grads_in, grads, sem.at[0])]
     parts, at = [], 0
     for k, ref in enumerate((gq, gkv, go, gup, gdn)):
         cols = pl.ds(at, ref.shape[1])
-        parts.append(pltpu.make_async_copy(grads.at[:, cols], ref, sem.at[3 + k]))
+        parts.append(pltpu.make_async_copy(grads.at[:, cols], ref, sem.at[1 + k]))
         at += ref.shape[1]
-    back = [
-        parts,
-        [pltpu.make_async_copy(held.at[0], out, sem.at[8])],
-        [pltpu.make_async_copy(held.at[1], gx, sem.at[9])],
-    ]
+    back = [parts]
+    for k, (src, dst) in enumerate(((out_in, out), (gx_in, gx))):
+        rows = src.shape[0] // 4
+        for j in range(4):
+            part, at = pl.ds(j * rows, rows), 6 + 2 * (4 * k + j)
+            there.append(pltpu.make_async_copy(src.at[part], held.at[k, part], sem.at[at]))
+            back.append([pltpu.make_async_copy(held.at[k, part], dst.at[part], sem.at[at + 1])])
+    for cp in there:
+        cp.start()
     t = lax.axis_index("tensor")
     n = g1.shape[0] // 128
     for k, ref in enumerate((g1, b1, g2, b2)):
@@ -1338,7 +1338,7 @@
         out_shape=shapes,
         in_specs=[hbm, hbm, hbm, vm, vm],
         out_specs=[hbm if len(shape.shape) > 1 else vm for shape in shapes],
-        scratch_shapes=[VMEM((2, T, D), BF), VMEM((R, n_grads), F32), DMA((10,))],
+        scratch_shapes=[VMEM((2, T, D), BF), VMEM((R, n_grads), F32), DMA((22,))],
         compiler_params=pltpu.CompilerParams(vmem_limit_bytes=VMEM_LIMIT),
         name="finish",
     )(out, gx, grads, early, late)

time: 155 us -> 152 us (0.981)
  Pallas kernels: 154 us -> 151 us
    pallas_call x1, Pallas kernels: 149 us -> 146 us  [token_plan(): pl.pallas_call(partial(block_kernel, dims), out_shape=[s((T, D), BF), s((...]
where the time goes in v1:
time: 152 us
  Pallas kernels  151 us (99%)
    pallas_call x1, Pallas kernels, token_plan(): pl.pallas_call(partial(block_kernel, dims), out_shape=[s((T, D), BF), s((...  146 us
    pallas_call x1, Pallas kernels, token_plan(): pl.pallas_call(partial(finish_kernel, dims), out_shape=shapes, in_specs=[...  4.58 us

profile of v1, /device:TPU:0, one launch (start us, length us, event | category | flops | bytes accessed | tf_op | source)
XLA Modules:
  0.0 151.6 jit_solution(12101648615691748825)
XLA Ops:
  0.7 146.1 %block.1 = (bf16[1024,768]{1,0:T(8,128)(2,1)}, bf16[1024,768]{1,0:T(8,128)(2,1)}, bf16[6,2,4,2,2,48,512]{6,5,4,3,2,1,0:T(8,128)(2,1)}, f32[48,3968]{1,0:T(8,128)}, f32[32,128]{1,0:T(8,128)}, /*index=5*/f32[32,128]{1,0:T(8,128)}) custom-call(bf16[1024,768]{1,0:T(8,128)(2,1)} %bitcast.13, bf16[1024,768]{1,0:T(8,128)(2,1)} %bitcast.14, s32[2]{0:T(128)} %bitcast.17, ...), custom_call_target="tpu_custom_call" | custom-call | tf_op jit(solution)/shard_map/block/pallas_call | solution.py:1242
  146.8 4.6 %finish.1 = (bf16[1024,768]{1,0:T(8,128)(2,1)}, bf16[1024,768]{1,0:T(8,128)(2,1)}, f32[768]{0:T(1024)}, f32[768]{0:T(1024)}, f32[768]{0:T(1024)}, /*index=5*/f32...) custom-call(bf16[1024,768]{1,0:T(8,128)(2,1)} %get-tuple-element.37., ...), custom_call_target="tpu_custom_call" | custom-call | tf_op jit(solution)/shard_map/finish/pallas_call | solution.py:1336

commit v2 on v1

--- a/solution.py
+++ b/solution.py
@@ -1120,13 +1120,13 @@
         sums[5:6, 0:128] += jnp.sum(dkvb.astype(F32), axis=0, keepdims=True)
 
     input_grad(0)
+    red.run(LAST_SUMS[1])
+    input_grad(1)
     own_dkv(1)
-    red.run(LAST_SUMS[1])
     gkvs = tn(h1[...], dkvn[...]).astype(BF).reshape(ZC, XC, CC, R, 128)
     for t in range(2):
         gkv[t] = gkvs
     red.run([(last + thirds, 0)])
-    input_grad(1)
     input_grad(2)
     red.run(LAST_SUMS[2])
     input_grad(3)

time: 152 us -> 152 us (level)
  no operation moved by 1% of the time
where the time goes in v2:
time: 152 us
  Pallas kernels  151 us (99%)
    pallas_call x1, Pallas kernels, token_plan(): pl.pallas_call(partial(block_kernel, dims), out_shape=[s((T, D), BF), s((...  146 us
    pallas_call x1, Pallas kernels, token_plan(): pl.pallas_call(partial(finish_kernel, dims), out_shape=shapes, in_specs=[...  4.58 us

profile of v2, /device:TPU:0, one launch (start us, length us, event | category | flops | bytes accessed | tf_op | source)
XLA Modules:
  0.0 151.9 jit_solution(1868764259261138685)
XLA Ops:
  0.7 146.4 %block.1 = (bf16[1024,768]{1,0:T(8,128)(2,1)}, bf16[1024,768]{1,0:T(8,128)(2,1)}, bf16[6,2,4,2,2,48,512]{6,5,4,3,2,1,0:T(8,128)(2,1)}, f32[48,3968]{1,0:T(8,128)}, f32[32,128]{1,0:T(8,128)}, /*index=5*/f32[32,128]{1,0:T(8,128)}) custom-call(bf16[1024,768]{1,0:T(8,128)(2,1)} %bitcast.13, bf16[1024,768]{1,0:T(8,128)(2,1)} %bitcast.14, s32[2]{0:T(128)} %bitcast.17, ...), custom_call_target="tpu_custom_call" | custom-call | tf_op jit(solution)/shard_map/block/pallas_call | solution.py:1242
  147.1 4.6 %finish.1 = (bf16[1024,768]{1,0:T(8,128)(2,1)}, bf16[1024,768]{1,0:T(8,128)(2,1)}, f32[768]{0:T(1024)}, f32[768]{0:T(1024)}, f32[768]{0:T(1024)}, /*index=5*/f32...) custom-call(bf16[1024,768]{1,0:T(8,128)(2,1)} %get-tuple-element.37., ...), custom_call_target="tpu_custom_call" | custom-call | tf_op jit(solution)/shard_map/finish/pallas_call | solution.py:1336
